TPU v7x, 128 devices: a whole 4x4x4 slice. The times are simulated.
128 devices in a mesh: wide: 16 (over z, x), narrow: 8 (over y, core).
Axes of the slice: x: 4, y: 4, z: 4, core: 2. Of those that a mesh axis runs over, the one named last changes fastest.
Arguments:
- cotangent: float32 [1536, 256, 256], P(('wide', 'narrow')), may hold values from -6 to 6
- row_basis: float32 [1536, 256, 128], P(('wide', 'narrow')), may hold values from -0.375 to 0.375
- col_basis: float32 [1536, 256, 128], P(('wide', 'narrow')), may hold values from -0.5 to 0.5
- leaf_up: float32 [1536, 128, 128], P(('wide', 'narrow')), may hold values from -0.15625 to 0.15625
- node_up: float32 [128, 128, 128], P(('wide', 'narrow')), may hold values from -0.1875 to 0.1875
- node_couple: float32 [128, 2, 128, 128], P(('wide', 'narrow')), may hold values from -0.375 to 0.375
- group_couple: float32 [16, 8, 128, 128], P('wide', 'narrow'), may hold values from -0.1875 to 0.1875
- node_down: float32 [128, 128, 128], P(('wide', 'narrow')), may hold values from -0.5 to 0.5
- leaf_down: float32 [1536, 128, 128], P(('wide', 'narrow')), may hold values from -0.5 to 0.5
- near_blocks: float32 [1536, 4, 256, 256], P(('wide', 'narrow')), may hold values from -0.1875 to 0.1875
- near_index: int32 [1536, 4], P(('wide', 'narrow')), may hold values from 0 to 1535, as said below
- far_nodes: int32 [128, 2], P(('wide', 'narrow')), may hold values from 0 to 7, as said below
- far_groups: int32 [16, 8], P('wide', 'narrow'), may hold values from 0 to 15, as said below
Outputs:
- product: float32 [1536, 256, 256], P(('wide', 'narrow'))
Inputs may be any that keep to these rules, and one draw needn't show every extreme that they name: near_index[l, 0] is l; every other entry differs from l by 1 to 2. far_nodes[d, j] never equals d % 8; the entries of a row differ. far_groups[g, j] never equals g; the entries of a row differ.
All inputs are finite; a program needn't handle non-finite values.
Results may differ from a plain program's by a relative error of at most 0.000062.
Values sent between devices are 32-bit elements; how exact they have to be, the bound alone decides.
A program may use at most 128 MiB of HBM per device.

v0:
```python
import jax
import jax.numpy as jnp
from jax import lax
from jax.sharding import PartitionSpec as P

NEAR_REACH = 2
HIGH = lax.Precision.HIGHEST


def from_behind(value, axis, steps):
    count = lax.axis_size(axis)
    leading, last = (max(0, -steps), min(count, count - steps))
    return lax.ppermute(value, axis, [(source, source + steps) for source in range(leading, last)])


def shards(
    cotangent,
    row_basis,
    col_basis,
    leaf_up,
    node_up,
    node_couple,
    group_couple,
    node_down,
    leaf_down,
    near_blocks,
    near_index,
    far_nodes,
    far_groups,
):
    leaves = cotangent.shape[0]
    lower = from_behind(cotangent[leaves - NEAR_REACH :], ("wide", "narrow"), 1)
    upper = from_behind(cotangent[:NEAR_REACH], ("wide", "narrow"), -1)
    leaf_coeffs = jnp.einsum("lpk,lpv->lkv", row_basis, cotangent, precision=HIGH)
    node_coeffs = jnp.einsum("lkm,lkv->mv", leaf_up, leaf_coeffs, precision=HIGH)
    up_term = jnp.dot(node_up[0].T, node_coeffs, precision=HIGH)
    siblings = lax.all_gather(node_coeffs[None], "narrow", axis=0, tiled=True)
    group_coeffs = lax.psum(up_term, "narrow")
    picked = siblings[far_nodes[0]]
    node_out = jnp.einsum("jkm,jkv->mv", node_couple[0], picked, precision=HIGH)
    all_groups = lax.all_gather(group_coeffs[None], "wide", axis=0, tiled=True)
    picked_groups = all_groups[far_groups[0]]
    partial_value = jnp.einsum("jkm,jkv->mv", group_couple[0], picked_groups, precision=HIGH)
    group_out = lax.psum(partial_value, "narrow")
    node_total = node_out + jnp.dot(node_down[0], group_out, precision=HIGH)
    leaf_total = jnp.einsum("lmk,kv->lmv", leaf_down, node_total, precision=HIGH)
    far_part = jnp.einsum("lpk,lkv->lpv", col_basis, leaf_total, precision=HIGH)
    extended = jnp.concatenate([lower, cotangent, upper], axis=0)
    node_rank = lax.axis_index("wide") * lax.axis_size("narrow") + lax.axis_index("narrow")
    first_leaf = node_rank * leaves - NEAR_REACH
    local_index = near_index - first_leaf
    sources = extended[local_index]
    near_part = jnp.einsum("ljpq,ljpv->lqv", near_blocks, sources, precision=HIGH)
    return far_part + near_part


def solution(mesh):
    in_specs = (
        P(("wide", "narrow"), None, None),
        P(("wide", "narrow"), None, None),
        P(("wide", "narrow"), None, None),
        P(("wide", "narrow"), None, None),
        P(("wide", "narrow"), None, None),
        P(("wide", "narrow"), None, None, None),
        P("wide", "narrow", None, None),
        P(("wide", "narrow"), None, None),
        P(("wide", "narrow"), None, None),
        P(("wide", "narrow"), None, None, None),
        P(("wide", "narrow"), None),
        P(("wide", "narrow"), None),
        P("wide", "narrow"),
    )
    out_specs = P(("wide", "narrow"), None, None)
    return jax.shard_map(shards, mesh=mesh, in_specs=in_specs, out_specs=out_specs, check_vma=False)
```

profile of v0, /device:TPU:0, one launch (start us, length us, event | category | flops | bytes accessed | tf_op | source)
XLA Modules:
  0.0 259.9 jit_solution(13110974289088481287)
XLA Ops:
  6.5 7.7 %fusion.14 = f32[12,128,256]{1,2,0:T(8,128)S(1)} fusion(f32[12,256,128]{2,1,0:T(8,128)} %param.14, f32[12,256,256]{2,1,0:T(8,128)} %param.13), kind=kOutput, calls=%fused_computation.26 | convolution fusion | flops 1207959552 | bytes 6291456 | tf_op jit(solution)/shard_map/lpk,lpv->lkv/dot_general | solution.py:34
  14.3 1.4 fusion.15
  15.7 0.9 convolution_bitcast_fusion.2
  16.7 0.7 all-gather.6.cloned.1.call-update
  17.5 61.0 %all-reduce.3.cloned.1.call-done = f32[1,128,256]{1,2,0:T(8,128)} async-done(((f32[1,128,256]{1,2,0:T(8,128)}), f32[1,128,256]{1,2,0:T(8,128)}) %all-reduce.3.cloned.1.call-update) | async-done | bytes 131088 | tf_op jit(solution)/shard_map/psum | solution.py:38
  78.5 1.7 copy.25
  80.2 2.1 fusion.13
  82.3 1.3 collective-permute-start
  83.7 1.5 collective-permute-start.1
  86.1 1.4 collective-permute-done.1
  87.5 4.3 %pad_maximum_fusion = f32[16,256,256]{2,1,0:T(8,128)} fusion(f32[2,256,256]{2,1,0:T(8,128)S(1)} %collective-permute-done.1, f32[12,256,256]{2,1,0:T(8,128)} %param.13, f32[2,256,256]{2,1,0:T(8,128)S(1)} %collective-permute-done), kind=kLoop, calls=%fused_computation.2 | loop fusion | flops 2097152 | bytes 8388608 | tf_op jit(solution)/shard_map/concatenate | solution.py:48
  91.7 10.0 %gather_fusion.1 = f32[48,256,256]{2,1,0:T(8,128)} fusion(f32[16,256,256]{2,1,0:T(8,128)} %pad_maximum_fusion, s32[1024]{0:T(1024)S(1)} %pad_clamp_fusion), kind=kCustom, calls=%fused_computation.1 | custom fusion | bytes 25166016 | tf_op jit(solution)/shard_map/gather | solution.py:52
  101.8 5.8 %all-gather.6.cloned.1.call-done = f32[1024,256]{0,1:T(8,128)} async-done(((f32[128,256]{0,1:T(8,128)}), f32[1024,256]{0,1:T(8,128)}) %all-gather.6.cloned.1.call-update) | async-done | bytes 1048592 | tf_op jit(solution)/shard_map/all_gather | solution.py:37
  107.6 1.6 copy.34
  109.2 0.6 gather_fusion
  109.7 45.5 %all-gather.4.cloned.1.call-done = f32[16,128,256]{2,1,0:T(8,128)} async-done(((f32[1,128,256]{2,1,0:T(8,128)}), f32[16,128,256]{2,1,0:T(8,128)}) %all-gather.4.cloned.1.call-update) | async-done | bytes 2097168 | tf_op jit(solution)/shard_map/all_gather | solution.py:41
  155.2 1.9 convolution_bitcast_fusion.1
  157.2 0.6 convolution_bitcast_fusion
  157.8 58.3 %all-reduce.5.cloned.1.call-done = f32[128,256]{0,1:T(8,128)} async-done(((f32[128,256]{0,1:T(8,128)}), f32[128,256]{0,1:T(8,128)}) %all-reduce.5.cloned.1.call-update) | async-done | bytes 131088 | tf_op jit(solution)/shard_map/psum | solution.py:44
  216.1 1.2 fusion.3
  217.3 2.5 fusion.16
  219.9 2.9 %fusion.1 = f32[12,256,256]{2,1,0:T(8,128)S(1)} fusion(f32[12,256,128]{2,1,0:T(8,128)S(1)} %copy-done, f32[256,12,128]{2,0,1:T(8,128)S(1)} %fusion.16), kind=kOutput, calls=%fused_computation.5 | convolution fusion | flops 1207959552 | bytes 6291456 | tf_op jit(solution)/shard_map/lpk,lkv->lpv/dot_general | solution.py:47
  222.8 27.0 %fusion = f32[12,256,256]{1,2,0:T(8,128)} fusion(f32[12,256,256]{2,1,0:T(8,128)S(1)} %fusion.1, f32[12,4,256,256]{3,2,1,0:T(8,128)} %bitcast.62, f32[12,4,256,256]{3,2,1,0:T(8,128)} %param.22), kind=kOutput, calls=%fused_computation.4 | convolution fusion | flops 9664462848 | bytes 31457280 | tf_op jit(solution)/shard_map/ljpq,ljpv->lqv/dot_general | solution.py:53
  249.8 3.5 %copy.28 = f32[12,256,256]{2,1,0:T(8,128)} copy(f32[12,256,256]{1,2,0:T(8,128)} %fusion) | data formatting | bytes 6291456 | tf_op jit(solution)/shard_map/add | solution.py:54
  (32 shorter events, 0.4 us)
Async XLA Ops:
  6.5 213.3 %copy-start = (f32[12,256,128]{2,1,0:T(8,128)S(1)}, f32[12,256,128]{2,1,0:T(8,128)}, u32[]{:S(2)}) copy-start(f32[12,256,128]{2,1,0:T(8,128)} %param.15) | copy-start | bytes 4718596
  6.5 7.7 %copy-start.2 = (f32[12,128,128]{2,1,0:T(8,128)S(1)}, f32[12,128,128]{2,1,0:T(8,128)}, u32[]{:S(2)}) copy-start(f32[12,128,128]{2,1,0:T(8,128)} %param.16) | copy-start | bytes 2359300
  6.5 9.2 %copy-start.4 = (f32[1,128,128]{2,1,0:T(8,128)S(1)}, f32[1,128,128]{2,1,0:T(8,128)}, u32[]{:S(2)}) copy-start(f32[1,128,128]{2,1,0:T(8,128)} %param.17) | copy-start | bytes 196612
  6.5 72.0 %all-reduce.3.cloned.1.call-start = ((), (), s32[]{:S(2)}) async-start(), calls=%async_computation | async-start | bytes 262144 | tf_op jit(solution)/shard_map/psum | solution.py:38
  14.3 70.9 %copy-start.7 = (s32[12,4]{0,1:T(4,128)S(1)}, s32[12,4]{0,1:T(4,128)}, u32[]{:S(2)}) copy-start(s32[12,4]{0,1:T(4,128)} %param.23) | copy-start | bytes 580
  14.3 71.7 %copy-start.8 = (s32[1,2]{1,0:T(1,128)S(1)}, s32[1,2]{1,0:T(1,128)}, u32[]{:S(2)}) copy-start(s32[1,2]{1,0:T(1,128)} %param.24) | copy-start | bytes 28
  15.7 1.0 copy-start.1
  16.7 90.9 %all-gather.6.cloned.1.call-start = ((), (), s32[]{:S(2)}) async-start(), calls=%async_computation.3 | async-start | bytes 1179648 | tf_op jit(solution)/shard_map/all_gather | solution.py:37
  17.4 137.8 %all-gather.4.cloned.1.call-start = ((), (), s32[]{:S(2)}) async-start(), calls=%async_computation.1 | async-start | bytes 2228224 | tf_op jit(solution)/shard_map/all_gather | solution.py:41
  80.2 135.9 %all-reduce.5.cloned.1.call-start = ((), (), s32[]{:S(2)}) async-start(), calls=%async_computation.2 | async-start | bytes 262144 | tf_op jit(solution)/shard_map/psum | solution.py:44
  82.3 3.7 %collective-permute-start = (f32[2,256,256]{2,1,0:T(8,128)}, f32[2,256,256]{2,1,0:T(8,128)S(1)}, u32[]{:S(2)}, u32[]{:S(2)}) collective-permute-start(f32[2,256,256]{2,1,0:T(8,128)} %get-tuple-element.16), channel_id=1, source_target_pairs={{0,1},{1,2},{2,3},{3,4},{4,5},{5,6},{6,7},{7,8},{8,9},{9,10},{10,1... | collective-permute-start | bytes 1572872 | tf_op jit(solution)/shard_map/ppermute | solution.py:13
  83.7 3.8 %collective-permute-start.1 = (f32[2,256,256]{2,1,0:T(8,128)S(1)}, f32[2,256,256]{2,1,0:T(8,128)S(1)}, u32[]{:S(2)}, u32[]{:S(2)}) collective-permute-start(f32[2,256,256]{2,1,0:T(8,128)S(1)} %get-tuple-element.17), channel_id=1, source_target_pairs={{1,0},{2,1},{3,2},{4,3},{5,4},{6,5},{7,6},{8,7},{9,8},{10,9},{11,1... | collective-permute-start | bytes 1572872 | tf_op jit(solution)/shard_map/ppermute | solution.py:13
  91.7 63.5 %copy-start.5 = (f32[1,1,128,128]{3,2,1,0:T(8,128)S(1)}, f32[1,1,128,128]{3,2,1,0:T(8,128)}, u32[]{:S(2)}) copy-start(f32[1,1,128,128]{3,2,1,0:T(8,128)} %param.19) | copy-start | bytes 196612
  101.8 55.5 %copy-start.3 = (f32[1,2,128,128]{3,2,1,0:T(8,128)S(1)}, f32[1,2,128,128]{3,2,1,0:T(8,128)}, u32[]{:S(2)}) copy-start(f32[1,2,128,128]{3,2,1,0:T(8,128)} %param.18) | copy-start | bytes 393220
  101.8 114.4 %copy-start.6 = (f32[1,128,128]{2,1,0:T(8,128)S(1)}, f32[1,128,128]{2,1,0:T(8,128)}, u32[]{:S(2)}) copy-start(f32[1,128,128]{2,1,0:T(8,128)} %param.20) | copy-start | bytes 196612
Sparse Core Ops, SparseCore 0:
  16.8 61.6 all-reduce.2
  80.3 27.2 all-gather.5
  110.0 45.2 all-gather.3
  157.5 58.5 all-reduce.4
where the time goes:
time: 260 us
  waiting for transfers between devices  173 us (67%)
  matrix products  46.2 us (18%)
  local copies, waits for them, and re-layouts  19.7 us (8%)
  between operations  14 us (5%)
  other arithmetic  4.28 us (2%)
  starting transfers between devices  2.91 us (1%)
    psum x1, waiting for transfers between devices, shards(): group_coeffs = lax.psum(up_term, 'narrow')  61 us
    psum x1, waiting for transfers between devices, shards(): group_out = lax.psum(partial_value, 'narrow')  58.3 us
    all_gather x1, waiting for transfers between devices, shards(): all_groups = lax.all_gather(group_coeffs[None], 'wide', axis=0, tiled=True)  45.5 us
    dot_general x1, matrix products, shards(): jnp.einsum('ljpq,ljpv->lqv', near_blocks, sources, precision=HIGH)  27 us
    gather x1, local copies, waits for them, and re-layouts, shards(): sources = extended[local_index]  10 us
    dot_general x1, matrix products, shards(): jnp.einsum('lpk,lpv->lkv', row_basis, cotangent, precision=HIGH)  7.71 us
    all_gather x1, waiting for transfers between devices, shards(): siblings = lax.all_gather(node_coeffs[None], 'narrow', axis=0, tiled=True)  5.84 us
  transfers between devices with their start and end apart: 6, of which 5 were waited for; matrix products, arithmetic and copies ran while one was open for 8% of the time, Pallas kernels for 0%

commit v1 on v0

--- a/solution.py
+++ b/solution.py
@@ -34,7 +34,11 @@
     leaf_coeffs = jnp.einsum("lpk,lpv->lkv", row_basis, cotangent, precision=HIGH)
     node_coeffs = jnp.einsum("lkm,lkv->mv", leaf_up, leaf_coeffs, precision=HIGH)
     up_term = jnp.dot(node_up[0].T, node_coeffs, precision=HIGH)
-    siblings = lax.all_gather(node_coeffs[None], "narrow", axis=0, tiled=True)
+    block = node_coeffs[None]
+    count_2 = lax.axis_size("narrow")
+    blocks = jnp.stack([block for _ in range(count_2)])
+    blocks = lax.all_to_all(blocks, "narrow", split_axis=0, concat_axis=0)
+    siblings = jnp.concatenate(blocks, axis=0)
     group_coeffs = lax.psum(up_term, "narrow")
     picked = siblings[far_nodes[0]]
     node_out = jnp.einsum("jkm,jkv->mv", node_couple[0], picked, precision=HIGH)

time: 260 us -> 230 us (0.88)
  waiting for transfers between devices: 173 us -> 139 us
  starting transfers between devices: 2.91 us -> 7.39 us
    all_gather x1, waiting for transfers between devices: 45.5 us -> 15.4 us  [shards(): all_groups = lax.all_gather(group_coeffs[None], 'wide', axis=0, tiled=True)]
    all_gather x1 -> x0, waiting for transfers between devices: 5.84 us -> none  [shards(): siblings = lax.all_gather(node_coeffs[None], 'narrow', axis=0, tiled=True)]
    all_to_all x0 -> x1, starting transfers between devices: none -> 3.56 us  [shards(): blocks = lax.all_to_all(blocks, 'narrow', split_axis=0, concat_axis=0)]
  transfers between devices with their start and end apart: 6 -> 6, of which waited for: 5 -> 4; matrix products, arithmetic and copies ran while one was open for 8% -> 8% of each run, Pallas kernels for 0% -> 0%
where the time goes in v1:
time: 230 us
  waiting for transfers between devices  139 us (60%)
  matrix products  46.2 us (20%)
  local copies, waits for them, and re-layouts  19.3 us (8%)
  between operations  14 us (6%)
  starting transfers between devices  7.39 us (3%)
  other arithmetic  4.46 us (2%)
    psum x1, waiting for transfers between devices, shards(): group_coeffs = lax.psum(up_term, 'narrow')  61.8 us
    psum x1, waiting for transfers between devices, shards(): group_out = lax.psum(partial_value, 'narrow')  58.5 us
    dot_general x1, matrix products, shards(): jnp.einsum('ljpq,ljpv->lqv', near_blocks, sources, precision=HIGH)  27 us
    all_gather x1, waiting for transfers between devices, shards(): all_groups = lax.all_gather(group_coeffs[None], 'wide', axis=0, tiled=True)  15.4 us
    gather x1, local copies, waits for them, and re-layouts, shards(): sources = extended[local_index]  9.91 us
    dot_general x1, matrix products, shards(): jnp.einsum('lpk,lpv->lkv', row_basis, cotangent, precision=HIGH)  7.71 us
  transfers between devices with their start and end apart: 6, of which 4 were waited for; matrix products, arithmetic and copies ran while one was open for 8% of the time, Pallas kernels for 0%

profile of v1, /device:TPU:0, one launch (start us, length us, event | category | flops | bytes accessed | tf_op | source)
XLA Modules:
  0.0 230.0 jit_solution(17238791322925021657)
XLA Ops:
  6.5 7.7 %fusion.14 = f32[12,128,256]{1,2,0:T(8,128)S(1)} fusion(f32[12,256,128]{2,1,0:T(8,128)} %param.14, f32[12,256,256]{2,1,0:T(8,128)} %param.13), kind=kOutput, calls=%fused_computation.26 | convolution fusion | flops 1207959552 | bytes 6291456 | tf_op jit(solution)/shard_map/lpk,lpv->lkv/dot_general | solution.py:34
  14.3 1.4 fusion.15
  15.7 0.9 convolution_bitcast_fusion.2
  16.7 61.8 %all-reduce.3.cloned.1.call-done = f32[1,128,256]{1,2,0:T(8,128)} async-done(((f32[1,128,256]{1,2,0:T(8,128)}), f32[1,128,256]{1,2,0:T(8,128)}) %all-reduce.3.cloned.1.call-update) | async-done | bytes 131088 | tf_op jit(solution)/shard_map/psum | solution.py:42
  78.5 1.7 copy.41
  80.3 1.1 stack.3
  81.3 3.6 %all-to-all-start = ((f32[8,1,128,256]{3,2,1,0:T(8,128)}), f32[8,1,128,256]{3,2,1,0:T(8,128)S(1)}, u32[]{:S(2)}, u32[]{:S(2)}) async-start(f32[8,1,128,256]{3,2,1,0:T(8,128)} %stack.3), calls=%async_computation | async-start | bytes 2097152 | tf_op jit(solution)/shard_map/all_to_all | solution.py:40
  85.0 2.3 fusion.13
  87.3 2.3 collective-permute-start
  89.5 1.5 collective-permute-start.1
  91.7 0.1 copy.42
  92.0 2.9 %collective-permute-done.1 = f32[2,256,256]{2,1,0:T(8,128)} collective-permute-done((f32[2,256,256]{2,1,0:T(8,128)}, f32[2,256,256]{2,1,0:T(8,128)}, u32[]{:S(2)}, u32[]{:S(2)}) %collective-permute-start.1) | collective-permute-done | bytes 524320 | tf_op jit(solution)/shard_map/ppermute | solution.py:13
  94.8 4.4 %pad_maximum_fusion = f32[16,256,256]{2,1,0:T(8,128)} fusion(f32[2,256,256]{2,1,0:T(8,128)} %collective-permute-done.1, f32[12,256,256]{2,1,0:T(8,128)} %param.13, f32[2,256,256]{2,1,0:T(8,128)S(1)} %collective-permute-done), kind=kLoop, calls=%fused_computation.2 | loop fusion | flops 2097152 | bytes 8388608 | tf_op jit(solution)/shard_map/concatenate | solution.py:52
  99.3 9.9 %gather_fusion.1 = f32[48,256,256]{2,1,0:T(8,128)} fusion(f32[16,256,256]{2,1,0:T(8,128)} %pad_maximum_fusion, s32[1024]{0:T(1024)S(1)} %pad_clamp_fusion), kind=kCustom, calls=%fused_computation.1 | custom fusion | bytes 25166016 | tf_op jit(solution)/shard_map/gather | solution.py:56
  109.2 0.6 gather_fusion
  109.7 15.4 %all-gather.2.cloned.1.call-done = f32[16,128,256]{2,1,0:T(8,128)} async-done(((f32[1,128,256]{2,1,0:T(8,128)}), f32[16,128,256]{2,1,0:T(8,128)}) %all-gather.2.cloned.1.call-update) | async-done | bytes 2097168 | tf_op jit(solution)/shard_map/all_gather | solution.py:45
  125.2 1.9 convolution_bitcast_fusion.1
  127.2 0.6 convolution_bitcast_fusion
  127.8 58.5 %all-reduce.5.cloned.1.call-done = f32[128,256]{0,1:T(8,128)} async-done(((f32[128,256]{0,1:T(8,128)}), f32[128,256]{0,1:T(8,128)}) %all-reduce.5.cloned.1.call-update) | async-done | bytes 131088 | tf_op jit(solution)/shard_map/psum | solution.py:48
  186.2 1.2 fusion.3
  187.4 2.5 %fusion.16 = f32[256,12,128]{2,0,1:T(8,128)S(1)} fusion(f32[256,128,1]{1,0,2:T(8,128)S(1)} %fusion.3, f32[12,128,128]{2,1,0:T(8,128)} %param.21), kind=kOutput, calls=%fused_computation.28 | convolution fusion | flops 603979776 | bytes 2490368 | tf_op jit(solution)/shard_map/lmk,kv->lmv/dot_general | solution.py:50
  190.0 2.9 %fusion.1 = f32[12,256,256]{2,1,0:T(8,128)S(1)} fusion(f32[12,256,128]{2,1,0:T(8,128)S(1)} %copy-done, f32[256,12,128]{2,0,1:T(8,128)S(1)} %fusion.16), kind=kOutput, calls=%fused_computation.5 | convolution fusion | flops 1207959552 | bytes 6291456 | tf_op jit(solution)/shard_map/lpk,lkv->lpv/dot_general | solution.py:51
  192.9 27.0 %fusion = f32[12,256,256]{1,2,0:T(8,128)} fusion(f32[12,256,256]{2,1,0:T(8,128)S(1)} %fusion.1, f32[12,4,256,256]{3,2,1,0:T(8,128)} %bitcast.62, f32[12,4,256,256]{3,2,1,0:T(8,128)} %param.22), kind=kOutput, calls=%fused_computation.4 | convolution fusion | flops 9664462848 | bytes 31457280 | tf_op jit(solution)/shard_map/ljpq,ljpv->lqv/dot_general | solution.py:57
  219.9 3.5 %copy.44 = f32[12,256,256]{2,1,0:T(8,128)} copy(f32[12,256,256]{1,2,0:T(8,128)} %fusion) | data formatting | bytes 6291456 | tf_op jit(solution)/shard_map/add | solution.py:58
  (30 shorter events, 0.4 us)
Async XLA Ops:
  6.5 183.4 %copy-start = (f32[12,256,128]{2,1,0:T(8,128)S(1)}, f32[12,256,128]{2,1,0:T(8,128)}, u32[]{:S(2)}) copy-start(f32[12,256,128]{2,1,0:T(8,128)} %param.15) | copy-start | bytes 4718596
  6.5 7.7 %copy-start.1 = (f32[12,128,128]{2,1,0:T(8,128)S(1)}, f32[12,128,128]{2,1,0:T(8,128)}, u32[]{:S(2)}) copy-start(f32[12,128,128]{2,1,0:T(8,128)} %param.16) | copy-start | bytes 2359300
  6.5 9.1 %copy-start.3 = (f32[1,128,128]{2,1,0:T(8,128)S(1)}, f32[1,128,128]{2,1,0:T(8,128)}, u32[]{:S(2)}) copy-start(f32[1,128,128]{2,1,0:T(8,128)} %param.17) | copy-start | bytes 196612
  6.5 72.0 %all-reduce.3.cloned.1.call-start = ((), (), s32[]{:S(2)}) async-start(), calls=%async_computation.1 | async-start | bytes 262144 | tf_op jit(solution)/shard_map/psum | solution.py:42
  16.6 74.4 %copy-start.6 = (s32[12,4]{0,1:T(4,128)S(1)}, s32[12,4]{0,1:T(4,128)}, u32[]{:S(2)}) copy-start(s32[12,4]{0,1:T(4,128)} %param.23) | copy-start | bytes 580
  16.6 75.3 %copy-start.7 = (s32[1,2]{1,0:T(1,128)S(1)}, s32[1,2]{1,0:T(1,128)}, u32[]{:S(2)}) copy-start(s32[1,2]{1,0:T(1,128)} %param.24) | copy-start | bytes 28
  16.6 108.6 %all-gather.2.cloned.1.call-start = ((), (), s32[]{:S(2)}) async-start(), calls=%async_computation.2 | async-start | bytes 2228224 | tf_op jit(solution)/shard_map/all_gather | solution.py:45
  81.3 27.8 %all-to-all-start = ((f32[8,1,128,256]{3,2,1,0:T(8,128)}), f32[8,1,128,256]{3,2,1,0:T(8,128)S(1)}, u32[]{:S(2)}, u32[]{:S(2)}) async-start(f32[8,1,128,256]{3,2,1,0:T(8,128)} %stack.3), calls=%async_computation | async-start | bytes 2097152 | tf_op jit(solution)/shard_map/all_to_all | solution.py:40
  84.9 101.3 %all-reduce.5.cloned.1.call-start = ((), (), s32[]{:S(2)}) async-start(), calls=%async_computation.3 | async-start | bytes 262144 | tf_op jit(solution)/shard_map/psum | solution.py:48
  87.3 4.7 %collective-permute-start = (f32[2,256,256]{2,1,0:T(8,128)}, f32[2,256,256]{2,1,0:T(8,128)S(1)}, u32[]{:S(2)}, u32[]{:S(2)}) collective-permute-start(f32[2,256,256]{2,1,0:T(8,128)} %get-tuple-element.16), channel_id=1, source_target_pairs={{0,1},{1,2},{2,3},{3,4},{4,5},{5,6},{6,7},{7,8},{8,9},{9,10},{10,1... | collective-permute-start | bytes 1572872 | tf_op jit(solution)/shard_map/ppermute | solution.py:13
  89.5 5.3 %collective-permute-start.1 = (f32[2,256,256]{2,1,0:T(8,128)}, f32[2,256,256]{2,1,0:T(8,128)}, u32[]{:S(2)}, u32[]{:S(2)}) collective-permute-start(f32[2,256,256]{2,1,0:T(8,128)} %get-tuple-element.17), channel_id=1, source_target_pairs={{1,0},{2,1},{3,2},{4,3},{5,4},{6,5},{7,6},{8,7},{9,8},{10,9},{11,1... | collective-permute-start | bytes 1572872 | tf_op jit(solution)/shard_map/ppermute | solution.py:13
  99.2 25.9 %copy-start.4 = (f32[1,1,128,128]{3,2,1,0:T(8,128)S(1)}, f32[1,1,128,128]{3,2,1,0:T(8,128)}, u32[]{:S(2)}) copy-start(f32[1,1,128,128]{3,2,1,0:T(8,128)} %param.19) | copy-start | bytes 196612
  99.2 27.9 %copy-start.2 = (f32[1,2,128,128]{3,2,1,0:T(8,128)S(1)}, f32[1,2,128,128]{3,2,1,0:T(8,128)}, u32[]{:S(2)}) copy-start(f32[1,2,128,128]{3,2,1,0:T(8,128)} %param.18) | copy-start | bytes 393220
  99.2 87.0 %copy-start.5 = (f32[1,128,128]{2,1,0:T(8,128)S(1)}, f32[1,128,128]{2,1,0:T(8,128)}, u32[]{:S(2)}) copy-start(f32[1,128,128]{2,1,0:T(8,128)} %param.20) | copy-start | bytes 196612
Sparse Core Ops, SparseCore 0:
  16.8 61.6 all-reduce.2
  80.9 44.2 all-gather.1
  127.6 58.5 all-reduce.4
